TPU v7x, 256 devices: a whole 4x4x8 slice. The times are simulated.
256 devices in a mesh: row: 32 (over y, z), col: 8 (over x, core).
Axes of the slice: x: 4, y: 4, z: 8, core: 2. Of those that a mesh axis runs over, the one named last changes fastest.
Arguments:
- factor: float32 [1, 32, 4, 8, 128, 128], P(None, 'row', None, 'col'), may hold values from -0.046875 to 0.046875
- pattern: int32 [1, 32, 4, 8], P(None, 'row', None, 'col'), may hold values 0 or 1
- inverse: float32 [32, 128, 128], replicated, may hold values from -2 to 2
- rhs: float32 [1, 32, 128, 128], P(None, 'row'), may hold values from -6 to 6
Outputs:
- forward_out: float32 [1, 32, 128, 128], P(None, 'row')
- backward_out: float32 [1, 32, 128, 128], P(None, 'row')
All inputs are finite; a program needn't handle non-finite values. No bound on the sum of `pattern` on one device may be relied on, other than what follows from the above.
Results may differ from a plain program's by a relative error of at most 0.0001.
Values sent between devices are 32-bit elements; how exact they have to be, the bound alone decides.
A program may use at most 64 MiB of HBM per device.

v0:
```python
import jax
import jax.numpy as jnp
from jax import lax
from jax.sharding import PartitionSpec as P


def shards(factor, pattern, inverse, rhs):
    row_count = lax.axis_size("row")
    col_count = lax.axis_size("col")
    row_index = lax.axis_index("row")
    col_index = lax.axis_index("col")
    topmost_level = lax.Precision.HIGHEST
    local_rows = factor.shape[0]
    local_cols = factor.shape[2]
    width = factor.shape[4]
    columns = rhs.shape[3]
    blocks_total = inverse.shape[0]
    level_count = blocks_total // col_count
    panel_blocks = factor.reshape(local_rows, local_cols, width, width)
    right = rhs.reshape(local_rows, width, columns)
    global_rows = jnp.arange(local_rows) * row_count + row_index
    row_levels = global_rows // col_count
    col_levels = jnp.arange(local_cols)
    lower = (row_levels[:, None] > col_levels[None, :]).astype(jnp.float32)
    active_blocks = pattern.reshape(local_rows, local_cols).astype(jnp.float32) * lower

    def forward(level, carry):
        solved, own_rows = carry
        offset = jnp.mod(row_index - level * col_count, row_count)
        valid = offset < col_count
        destination_row = level * col_count + jnp.minimum(offset, col_count - 1)
        row_slot = destination_row // row_count
        factor_row = lax.dynamic_index_in_dim(panel_blocks, row_slot, 0, keepdims=False)
        weight_matrix = lax.dynamic_index_in_dim(active_blocks, row_slot, 0, keepdims=False)
        owned_blocks = lax.dynamic_index_in_dim(
            solved.reshape(local_cols, col_count, width, columns), col_index, 1, keepdims=False
        )
        partial_result = jnp.einsum(
            "k,kab,kbr->ar", weight_matrix, factor_row, owned_blocks, precision=topmost_level
        )
        own_right = lax.dynamic_index_in_dim(right, row_slot, 0, keepdims=False)
        total = lax.psum(partial_result, "col")
        block_inverse = lax.dynamic_index_in_dim(inverse, destination_row, 0, keepdims=False)
        fresh = jnp.dot(block_inverse, own_right - total, precision=topmost_level)
        keeper = (valid & (offset == col_index)).astype(jnp.float32)
        picked = lax.psum(keeper * fresh, "row")
        solved = lax.dynamic_update_slice_in_dim(
            solved, picked[None], level * col_count + col_index, 0
        )
        previous = lax.dynamic_index_in_dim(own_rows, row_slot, 0, keepdims=False)
        stored = jnp.where(valid, fresh, previous)
        own_rows = stored[None]
        return (solved, own_rows)

    start_solved = jnp.zeros((blocks_total, width, columns), jnp.float32)
    start_own = jnp.zeros((local_rows, width, columns), jnp.float32)
    solved, own_rows = lax.fori_loop(0, level_count, forward, (start_solved, start_own))

    def backward(count, finished_blocks):
        level = level_count - 1 - count
        destination_row = level * col_count + col_index
        owner_row = destination_row % row_count
        factor_column_entries = lax.dynamic_index_in_dim(panel_blocks, level, 1, keepdims=False)
        weight_matrix = lax.dynamic_index_in_dim(active_blocks, level, 1, keepdims=False)
        owned_blocks = lax.dynamic_index_in_dim(
            finished_blocks.reshape(local_rows, row_count, width, columns),
            row_index,
            1,
            keepdims=False,
        )
        partial_result = jnp.einsum(
            "f,fcy,fch->yh",
            weight_matrix,
            factor_column_entries,
            owned_blocks,
            precision=topmost_level,
        )
        own_solved = lax.dynamic_index_in_dim(solved, destination_row, 0, keepdims=False)
        total = lax.psum(partial_result, "row")
        block_inverse = lax.dynamic_index_in_dim(inverse, destination_row, 0, keepdims=False)
        fresh = jnp.einsum("ab,ar->br", block_inverse, own_solved - total, precision=topmost_level)
        keeper = (owner_row == row_index).astype(jnp.float32)
        picked = lax.psum(keeper * fresh, "col")
        offset = jnp.mod(row_index - level * col_count, row_count)
        place = level * col_count + jnp.minimum(offset, col_count - 1)
        finished_blocks = lax.dynamic_update_slice_in_dim(finished_blocks, picked[None], place, 0)
        return finished_blocks

    start_done = jnp.zeros((blocks_total, width, columns), jnp.float32)
    finished_blocks = lax.fori_loop(0, level_count, backward, start_done)
    forward_out = own_rows.reshape(local_rows, 1, width, columns)
    backward_out = lax.dynamic_index_in_dim(
        finished_blocks.reshape(local_rows, row_count, width, columns), row_index, 1, keepdims=True
    )
    return (forward_out, backward_out)


def solution(mesh):
    return jax.shard_map(
        shards,
        mesh=mesh,
        in_specs=(
            P(None, "row", None, "col", None, None),
            P(None, "row", None, "col"),
            P(),
            P(None, "row", None, None),
        ),
        out_specs=(P(None, "row", None, None), P(None, "row", None, None)),
        check_vma=False,
    )
```

profile of v0, /device:TPU:1, one launch (start us, length us, event | category | flops | bytes accessed | tf_op | source)
XLA Modules:
  0.0 1696.6 jit_solution(7910112289259169579)
XLA Ops:
  7.2 0.7 compare_select_fusion
  7.9 0.7 compare_select_fusion.1
  8.5 1.0 bitcast_multiply_fusion
  9.6 0.2 broadcast.39.clone
  9.8 837.4 %while.32 = (s32[]{:T(128)}, f32[32,128,128]{2,1,0:T(8,128)S(1)}, f32[1,128,128]{2,1,0:T(8,128)S(1)}, s32[]{:T(128)}, s32[]{:T(128)}, /*index=5*/f32[32,128,128]...) while((s32[]{:T(128)}, f32[32,128,128]{2,1,0:T(8,128)S(1)}, ...), condition=%wide.region_3.4_spmd, body=%wide.region_0.3_spmd.sunk | while | flops 125911056 | bytes 1901045 | solution.py:57
  9.9 0.0 all-reduce.5.cloned.1.call-start
  9.9 1.0 convolution_bitcast_fusion.2
  10.9 0.0 all-reduce.5.cloned.1.call-update
  11.0 0.0 all-reduce.7.cloned.1.call-start
  11.0 68.0 %all-reduce.5.cloned.1.call-done = f32[128,128]{1,0:T(8,128)} async-done(((f32[128,128]{1,0:T(8,128)}), f32[128,128]{1,0:T(8,128)}) %all-reduce.5.cloned.1.call-update) | async-done | bytes 65552 | tf_op jit(solution)/shard_map/while/body/eval_jaxpr/psum | solution.py:42
  79.1 1.7 fusion.36
  80.8 0.0 all-reduce.7.cloned.1.call-update
  80.8 138.8 %all-reduce.7.cloned.1.call-done = f32[1,128,128]{2,1,0:T(8,128)} async-done(((f32[1,128,128]{2,1,0:T(8,128)}), f32[1,128,128]{2,1,0:T(8,128)}) %all-reduce.7.cloned.1.call-update) | async-done | bytes 65552 | tf_op jit(solution)/shard_map/while/body/eval_jaxpr/psum | solution.py:46
  219.6 0.8 constant_dynamic-update-slice_fusion.4
  220.5 1.0 convolution_bitcast_fusion.2
  221.5 0.0 all-reduce.5.cloned.1.call-update
  221.5 0.0 all-reduce.7.cloned.1.call-start
  221.6 66.6 %all-reduce.5.cloned.1.call-done = f32[128,128]{1,0:T(8,128)} async-done(((f32[128,128]{1,0:T(8,128)}), f32[128,128]{1,0:T(8,128)}) %all-reduce.5.cloned.1.call-update) | async-done | bytes 65552 | tf_op jit(solution)/shard_map/while/body/eval_jaxpr/psum | solution.py:42
  288.2 1.7 fusion.36
  289.9 138.6 %all-reduce.7.cloned.1.call-done = f32[1,128,128]{2,1,0:T(8,128)} async-done(((f32[1,128,128]{2,1,0:T(8,128)}), f32[1,128,128]{2,1,0:T(8,128)}) %all-reduce.7.cloned.1.call-update) | async-done | bytes 65552 | tf_op jit(solution)/shard_map/while/body/eval_jaxpr/psum | solution.py:46
  428.6 0.8 constant_dynamic-update-slice_fusion.4
  429.4 1.0 convolution_bitcast_fusion.2
  430.5 0.0 all-reduce.7.cloned.1.call-start
  430.6 66.3 %all-reduce.5.cloned.1.call-done = f32[128,128]{1,0:T(8,128)} async-done(((f32[128,128]{1,0:T(8,128)}), f32[128,128]{1,0:T(8,128)}) %all-reduce.5.cloned.1.call-update) | async-done | bytes 65552 | tf_op jit(solution)/shard_map/while/body/eval_jaxpr/psum | solution.py:42
  496.9 1.7 fusion.36
  498.6 138.6 %all-reduce.7.cloned.1.call-done = f32[1,128,128]{2,1,0:T(8,128)} async-done(((f32[1,128,128]{2,1,0:T(8,128)}), f32[1,128,128]{2,1,0:T(8,128)}) %all-reduce.7.cloned.1.call-update) | async-done | bytes 65552 | tf_op jit(solution)/shard_map/while/body/eval_jaxpr/psum | solution.py:46
  637.2 0.8 constant_dynamic-update-slice_fusion.4
  638.1 1.0 convolution_bitcast_fusion.2
  639.1 0.0 all-reduce.7.cloned.1.call-start
  639.2 66.6 %all-reduce.5.cloned.1.call-done = f32[128,128]{1,0:T(8,128)} async-done(((f32[128,128]{1,0:T(8,128)}), f32[128,128]{1,0:T(8,128)}) %all-reduce.5.cloned.1.call-update) | async-done | bytes 65552 | tf_op jit(solution)/shard_map/while/body/eval_jaxpr/psum | solution.py:42
  705.8 1.7 fusion.36
  707.6 138.8 %all-reduce.7.cloned.1.call-done = f32[1,128,128]{2,1,0:T(8,128)} async-done(((f32[1,128,128]{2,1,0:T(8,128)}), f32[1,128,128]{2,1,0:T(8,128)}) %all-reduce.7.cloned.1.call-update) | async-done | bytes 65552 | tf_op jit(solution)/shard_map/while/body/eval_jaxpr/psum | solution.py:46
  846.4 0.8 constant_dynamic-update-slice_fusion.4
  847.2 1.6 broadcast.39
  848.8 839.8 %while.33 = (s32[]{:T(128)}, f32[32,128,128]{2,1,0:T(8,128)}, s32[]{:T(128)}, s32[]{:T(128)}, f32[32,128,128]{2,1,0:T(8,128)}, /*index=5*/f32[32,128,128]{2,1,0:...) while((s32[]{:T(128)}, f32[32,128,128]{2,1,0:T(8,128)}, ...), condition=%wide.region_7.8_spmd, body=%wide.region_4.7_spmd.sunk | while | flops 50413572 | bytes 1379462 | solution.py:90
  848.8 0.6 constant_dynamic-slice_fusion.2
  849.4 2.4 fusion.40
  851.8 0.0 all-reduce.11.cloned.1.call-start
  851.8 139.6 %all-reduce.9.cloned.1.call-done = f32[128,128]{1,0:T(8,128)} async-done(((f32[128,128]{1,0:T(8,128)}), f32[128,128]{1,0:T(8,128)}) %all-reduce.9.cloned.1.call-update) | async-done | bytes 65552 | tf_op jit(solution)/shard_map/while/body/eval_jaxpr/psum | solution.py:79
  991.4 1.8 fusion.41
  993.3 65.0 %all-reduce.11.cloned.1.call-done = f32[1,128,128]{2,1,0:T(8,128)} async-done(((f32[1,128,128]{2,1,0:T(8,128)}), f32[1,128,128]{2,1,0:T(8,128)}) %all-reduce.11.cloned.1.call-update) | async-done | bytes 65552 | tf_op jit(solution)/shard_map/while/body/eval_jaxpr/psum | solution.py:83
  1058.3 1.5 constant_dynamic-update-slice_fusion.5
  1059.8 0.6 constant_dynamic-slice_fusion.2
  1060.4 2.4 fusion.40
  1062.7 0.0 all-reduce.11.cloned.1.call-start
  1062.8 138.3 %all-reduce.9.cloned.1.call-done = f32[128,128]{1,0:T(8,128)} async-done(((f32[128,128]{1,0:T(8,128)}), f32[128,128]{1,0:T(8,128)}) %all-reduce.9.cloned.1.call-update) | async-done | bytes 65552 | tf_op jit(solution)/shard_map/while/body/eval_jaxpr/psum | solution.py:79
  1201.1 1.8 fusion.41
  1203.0 65.0 %all-reduce.11.cloned.1.call-done = f32[1,128,128]{2,1,0:T(8,128)} async-done(((f32[1,128,128]{2,1,0:T(8,128)}), f32[1,128,128]{2,1,0:T(8,128)}) %all-reduce.11.cloned.1.call-update) | async-done | bytes 65552 | tf_op jit(solution)/shard_map/while/body/eval_jaxpr/psum | solution.py:83
  1268.0 1.5 constant_dynamic-update-slice_fusion.5
  1269.5 0.6 constant_dynamic-slice_fusion.2
  1270.1 2.4 fusion.40
  1272.4 0.0 all-reduce.11.cloned.1.call-start
  1272.5 138.3 %all-reduce.9.cloned.1.call-done = f32[128,128]{1,0:T(8,128)} async-done(((f32[128,128]{1,0:T(8,128)}), f32[128,128]{1,0:T(8,128)}) %all-reduce.9.cloned.1.call-update) | async-done | bytes 65552 | tf_op jit(solution)/shard_map/while/body/eval_jaxpr/psum | solution.py:79
  1410.8 1.8 fusion.41
  1412.7 65.0 %all-reduce.11.cloned.1.call-done = f32[1,128,128]{2,1,0:T(8,128)} async-done(((f32[1,128,128]{2,1,0:T(8,128)}), f32[1,128,128]{2,1,0:T(8,128)}) %all-reduce.11.cloned.1.call-update) | async-done | bytes 65552 | tf_op jit(solution)/shard_map/while/body/eval_jaxpr/psum | solution.py:83
  1477.7 1.5 constant_dynamic-update-slice_fusion.5
  1479.2 0.6 constant_dynamic-slice_fusion.2
  1479.8 2.4 fusion.40
  1482.2 0.0 all-reduce.11.cloned.1.call-start
  1482.2 138.0 %all-reduce.9.cloned.1.call-done = f32[128,128]{1,0:T(8,128)} async-done(((f32[128,128]{1,0:T(8,128)}), f32[128,128]{1,0:T(8,128)}) %all-reduce.9.cloned.1.call-update) | async-done | bytes 65552 | tf_op jit(solution)/shard_map/while/body/eval_jaxpr/psum | solution.py:79
  1620.2 1.8 fusion.41
  1622.1 65.0 %all-reduce.11.cloned.1.call-done = f32[1,128,128]{2,1,0:T(8,128)} async-done(((f32[1,128,128]{2,1,0:T(8,128)}), f32[1,128,128]{2,1,0:T(8,128)}) %all-reduce.11.cloned.1.call-update) | async-done | bytes 65552 | tf_op jit(solution)/shard_map/while/body/eval_jaxpr/psum | solution.py:83
  1687.1 1.5 constant_dynamic-update-slice_fusion.5
  1688.6 1.5 dynamic-slice_bitcast_fusion
  (25 shorter events, 0.2 us)
Async XLA Ops:
  7.2 2.7 copy-start.1
  9.9 69.2 %all-reduce.5.cloned.1.call-start = ((), (), s32[]{:S(2)}) async-start(), calls=%async_computation | async-start | bytes 131072 | tf_op jit(solution)/shard_map/while/body/eval_jaxpr/psum | solution.py:42
  11.0 208.7 %all-reduce.7.cloned.1.call-start = ((), (), s32[]{:S(2)}) async-start(), calls=%async_computation.1 | async-start | bytes 131072 | tf_op jit(solution)/shard_map/while/body/eval_jaxpr/psum | solution.py:46
  220.5 67.7 %all-reduce.5.cloned.1.call-start = ((), (), s32[]{:S(2)}) async-start(), calls=%async_computation | async-start | bytes 131072 | tf_op jit(solution)/shard_map/while/body/eval_jaxpr/psum | solution.py:42
  221.5 207.1 %all-reduce.7.cloned.1.call-start = ((), (), s32[]{:S(2)}) async-start(), calls=%async_computation.1 | async-start | bytes 131072 | tf_op jit(solution)/shard_map/while/body/eval_jaxpr/psum | solution.py:46
  429.4 67.4 %all-reduce.5.cloned.1.call-start = ((), (), s32[]{:S(2)}) async-start(), calls=%async_computation | async-start | bytes 131072 | tf_op jit(solution)/shard_map/while/body/eval_jaxpr/psum | solution.py:42
  430.5 206.8 %all-reduce.7.cloned.1.call-start = ((), (), s32[]{:S(2)}) async-start(), calls=%async_computation.1 | async-start | bytes 131072 | tf_op jit(solution)/shard_map/while/body/eval_jaxpr/psum | solution.py:46
  638.1 67.7 %all-reduce.5.cloned.1.call-start = ((), (), s32[]{:S(2)}) async-start(), calls=%async_computation | async-start | bytes 131072 | tf_op jit(solution)/shard_map/while/body/eval_jaxpr/psum | solution.py:42
  639.1 207.2 %all-reduce.7.cloned.1.call-start = ((), (), s32[]{:S(2)}) async-start(), calls=%async_computation.1 | async-start | bytes 131072 | tf_op jit(solution)/shard_map/while/body/eval_jaxpr/psum | solution.py:46
  847.2 1.6 copy-start
  848.8 142.6 %all-reduce.9.cloned.1.call-start = ((), (), s32[]{:S(2)}) async-start(), calls=%async_computation.2 | async-start | bytes 131072 | tf_op jit(solution)/shard_map/while/body/eval_jaxpr/psum | solution.py:79
  851.8 206.6 %all-reduce.11.cloned.1.call-start = ((), (), s32[]{:S(2)}) async-start(), calls=%async_computation.3 | async-start | bytes 131072 | tf_op jit(solution)/shard_map/while/body/eval_jaxpr/psum | solution.py:83
  1059.8 141.3 %all-reduce.9.cloned.1.call-start = ((), (), s32[]{:S(2)}) async-start(), calls=%async_computation.2 | async-start | bytes 131072 | tf_op jit(solution)/shard_map/while/body/eval_jaxpr/psum | solution.py:79
  1062.7 205.3 %all-reduce.11.cloned.1.call-start = ((), (), s32[]{:S(2)}) async-start(), calls=%async_computation.3 | async-start | bytes 131072 | tf_op jit(solution)/shard_map/while/body/eval_jaxpr/psum | solution.py:83
  1269.5 141.4 %all-reduce.9.cloned.1.call-start = ((), (), s32[]{:S(2)}) async-start(), calls=%async_computation.2 | async-start | bytes 131072 | tf_op jit(solution)/shard_map/while/body/eval_jaxpr/psum | solution.py:79
  1272.4 205.3 %all-reduce.11.cloned.1.call-start = ((), (), s32[]{:S(2)}) async-start(), calls=%async_computation.3 | async-start | bytes 131072 | tf_op jit(solution)/shard_map/while/body/eval_jaxpr/psum | solution.py:83
  1479.2 141.0 %all-reduce.9.cloned.1.call-start = ((), (), s32[]{:S(2)}) async-start(), calls=%async_computation.2 | async-start | bytes 131072 | tf_op jit(solution)/shard_map/while/body/eval_jaxpr/psum | solution.py:79
  1482.2 205.0 %all-reduce.11.cloned.1.call-start = ((), (), s32[]{:S(2)}) async-start(), calls=%async_computation.3 | async-start | bytes 131072 | tf_op jit(solution)/shard_map/while/body/eval_jaxpr/psum | solution.py:83
Sparse Core Ops, SparseCore 0:
  13.6 65.4 all-reduce.4
  83.5 136.0 all-reduce.6
  224.2 63.9 all-reduce.4
  292.5 136.0 all-reduce.6
  432.8 63.9 all-reduce.4
  501.1 136.0 all-reduce.6
  641.8 63.9 all-reduce.4
  710.3 136.0 all-reduce.6
  854.0 137.3 all-reduce.8
  994.3 63.9 all-reduce.10
  1065.0 136.0 all-reduce.8
  1204.0 63.9 all-reduce.10
  1274.7 136.0 all-reduce.8
  1413.7 63.9 all-reduce.10
  1484.1 136.0 all-reduce.8
  1623.1 63.9 all-reduce.10
where the time goes:
time: 1700 us
  waiting for transfers between devices  1640 us (96%)
  matrix products  27.5 us (2%)
    psum x4, waiting for transfers between devices, forward(): picked = lax.psum(keeper * fresh, 'row')  555 us
    psum x4, waiting for transfers between devices, backward(): total = lax.psum(partial_result, 'row')  554 us
    psum x4, waiting for transfers between devices, forward(): total = lax.psum(partial_result, 'col')  268 us
    psum x4, waiting for transfers between devices, backward(): picked = lax.psum(keeper * fresh, 'col')  260 us
  transfers between devices with their start and end apart: 16, of which 16 were waited for; matrix products, arithmetic and copies ran while one was open for 0% of the time, Pallas kernels for 0%

commit v1 on v0

v1 whole, which is shorter than its diff:
```python
import jax
import jax.numpy as jnp
from jax import lax
from jax.experimental import pallas as pl
from jax.experimental.pallas import tpu as pltpu
from jax.sharding import PartitionSpec as P

MESH = pl.DeviceIdType.MESH
F32 = jnp.float32
BF16 = jnp.bfloat16
LEVELS = 4
PER = 8
W = 128
S = W // PER
FAR_FIRST = (4, 3, 5, 2, 6, 1, 7, 0)


def halves(v):
    hi = v.astype(BF16)
    lo = (v - hi.astype(F32)).astype(BF16)
    return hi, lo


def quadrants(p, m, n):
    return p[:m, :n] + (p[m:, :n] + p[:m, n:])


def dot_nt(a, b):
    return lax.dot_general(a, b, (((1,), (1,)), ((), ())), preferred_element_type=F32)


def dot_nn(a, b):
    return lax.dot_general(a, b, (((1,), (0,)), ((), ())), preferred_element_type=F32)


def kernel(
    factor, pattern, inverse, rhs, y_out, x_out,
    d_in, l_in, b_in, b_t, m_in, m_hl, d_hl, dt_hl, y_in, p_in, y_own, u_own, t_own, y_all, u_all,
    load_sem, m_send, m_recv, m_relay, y_send, y_recv, p_send, p_recv, g_send, g_recv,
):
    row = lax.axis_index("row")
    col = lax.axis_index("col")
    level = row // PER
    z = row % PER
    x = col // 2
    h = col % 2

    def peer(dx, dh):
        return lax.rem(x + dx, 4) * 2 + lax.rem(h + dh, 2)

    col_peers = [peer(dx, dh) for dx, dh in ((2, 1), (2, 0), (1, 1), (3, 1), (1, 0), (3, 0), (0, 1))]

    load_d = pltpu.make_async_copy(inverse.at[row], d_in, load_sem.at[0])
    load_b = pltpu.make_async_copy(rhs.at[0, 0], b_in, load_sem.at[1])
    load_l = [pltpu.make_async_copy(factor.at[0, 0, k, 0], l_in.at[k], load_sem.at[2 + k]) for k in range(LEVELS - 1)]
    load_d.start()
    for k in range(LEVELS - 1):
        load_l[k].start()
    load_b.start()

    barrier = pltpu.get_barrier_semaphore()
    for dz in FAR_FIRST:
        for dy in (2, 1, 3):
            to = lax.rem(level + dy, LEVELS) * PER + lax.rem(z + dz, PER)
            pl.semaphore_signal(barrier, inc=1, device_id=(to, col), device_id_type=MESH)
    for c in col_peers:
        pl.semaphore_signal(barrier, inc=1, device_id=(row, c), device_id_type=MESH)

    load_d.wait()
    d = d_in[...]
    dh_, dl_ = halves(d)
    d_hl[:W, :] = dh_
    d_hl[W:, :] = dl_
    th, tl = halves(jnp.transpose(d))
    dt_hl[:W, :] = th
    dt_hl[W:, :] = tl
    for k in range(LEVELS - 1):
        load_l[k].wait()
        keep = jnp.where(level > k, pattern[0, k].astype(F32), 0.0)
        lh, ll = halves(l_in[k] * keep)
        m_in[k, col] = quadrants(dot_nn(d_hl[...], jnp.concatenate([lh, ll], axis=1)), W, W)
    load_b.wait()
    b_t[...] = jnp.transpose(b_in[...])
    bh, bl = halves(b_t[pl.ds(pl.multiple_of(col * S, S), S), :])
    start = quadrants(dot_nt(jnp.concatenate([bh, bl], axis=0), d_hl[...]), S, W)
    y_own[...] = start
    pl.semaphore_wait(barrier, 31)

    def wait(ref, sem):
        pltpu.make_async_copy(ref, ref, sem).wait()

    def send(src, dst, ssem, rsem, to_row, to_col):
        pltpu.make_async_remote_copy(
            src_ref=src, dst_ref=dst, send_sem=ssem, recv_sem=rsem, device_id=(to_row, to_col), device_id_type=MESH
        ).start()

    def to_level(src_of, dst, ssem, rsem, target):
        for dz in FAR_FIRST:
            zt = lax.rem(z + dz, PER)
            send(src_of(zt), dst, ssem, rsem, target * PER + zt, col)

    def to_col(own, dst, which):
        for c in col_peers:
            send(own, dst, g_send.at[which], g_recv.at[which], row, c)

    for lev in range(LEVELS):

        @pl.when(level == lev)
        def _(lev=lev):
            if lev == 0:
                for target in range(1, LEVELS):
                    to_level(lambda zt: y_own, y_in.at[0, z], y_send, y_recv.at[0], target)
            for k in range(lev):
                own = m_in.at[k, col]
                for i, dx in enumerate((2, 1, 3)):
                    send(own, own, m_send, m_recv.at[k, i], row, peer(dx, 0))
                send(own, own, m_send, m_relay.at[k], row, peer(0, 1))
            for k in range(lev):
                for i, dx in ((1, 1), (2, 3), (0, 2)):
                    got = m_in.at[k, peer(4 - dx, 0)]
                    wait(got, m_recv.at[k, i])
                    send(got, got, m_send, m_relay.at[k], row, peer(0, 1))
                wait(m_in.at[k, pl.ds(0, 4)], m_relay.at[k])
                for c in range(PER):
                    mh, ml = halves(m_in[k, c])
                    m_hl[k, :W, c * W:(c + 1) * W] = mh
                    m_hl[k, W:, c * W:(c + 1) * W] = ml
            acc = start
            for k in range(lev):
                wait(y_in.at[k], y_recv.at[k])
                parts = [halves(y_in[k, c]) for c in range(PER)]
                lhs = jnp.concatenate(
                    [jnp.concatenate([p[0] for p in parts], axis=1), jnp.concatenate([p[1] for p in parts], axis=1)], axis=0
                )
                acc = acc - quadrants(dot_nt(lhs, m_hl[k]), S, W)
            if lev > 0:
                y_own[...] = acc
                for target in range(lev + 1, LEVELS):
                    to_level(lambda zt: y_own, y_in.at[lev, z], y_send, y_recv.at[lev], target)
            if lev < LEVELS - 1:
                y_all[col] = acc
                to_col(y_own, y_all.at[col], 0)
            for up in range(LEVELS - 1, lev, -1):
                wait(p_in.at[up - 1], p_recv.at[up - 1])
                total = p_in[up - 1, 0]
                for c in range(1, PER):
                    total = total + p_in[up - 1, c]
                acc = acc - total
            u_own[...] = acc
            uh, ul = halves(acc)
            lhs = jnp.concatenate(
                [jnp.concatenate([uh, uh], axis=1), jnp.concatenate([ul, jnp.zeros_like(ul)], axis=1)], axis=0
            )
            for k in range(lev - 1, -1, -1):
                t = dot_nn(lhs, m_hl[k])
                t = t[:S] + t[S:]
                for c in range(PER):
                    t_own[k, c] = t[:, c * W:(c + 1) * W]
                to_level(lambda zt: t_own.at[k, zt], p_in.at[lev - 1, z], p_send, p_recv.at[lev - 1], k)
            if lev == LEVELS - 1:
                y_all[col] = acc
                to_col(y_own, y_all.at[col], 0)
            u_all[col] = acc
            to_col(u_own, u_all.at[col], 1)

            wait(y_all.at[pl.ds(0, PER - 1)], g_recv.at[0])
            y_out[0, 0] = jnp.transpose(y_all[...].reshape(W, W))
            wait(u_all.at[pl.ds(0, PER - 1)], g_recv.at[1])
            ah, al = halves(u_all[...].reshape(W, W))
            x_out[0, 0] = quadrants(dot_nt(dt_hl[...], jnp.concatenate([ah, al], axis=0)), W, W)

            for k in range(lev):
                wait(m_in.at[k, pl.ds(0, 7)], m_send)
                wait(t_own.at[k], p_send)
            for _ in range(lev + 1, LEVELS):
                wait(y_in.at[0], y_send)
            for which in range(2):
                wait(y_all.at[pl.ds(0, PER - 1)], g_send.at[which])


def shards(factor, pattern, inverse, rhs):
    out = jax.ShapeDtypeStruct((1, 1, W, W), F32)
    dma = pltpu.SemaphoreType.DMA
    return pl.pallas_call(
        kernel,
        out_shape=(out, out),
        in_specs=[
            pl.BlockSpec(memory_space=pltpu.HBM),
            pl.BlockSpec(memory_space=pltpu.SMEM),
            pl.BlockSpec(memory_space=pltpu.HBM),
            pl.BlockSpec(memory_space=pltpu.HBM),
        ],
        out_specs=(pl.BlockSpec(memory_space=pltpu.VMEM), pl.BlockSpec(memory_space=pltpu.VMEM)),
        scratch_shapes=[
            pltpu.VMEM((W, W), F32),
            pltpu.VMEM((LEVELS - 1, W, W), F32),
            pltpu.VMEM((W, W), F32),
            pltpu.VMEM((W, W), F32),
            pltpu.VMEM((LEVELS - 1, PER, W, W), F32),
            pltpu.VMEM((LEVELS - 1, 2 * W, PER * W), BF16),
            pltpu.VMEM((2 * W, W), BF16),
            pltpu.VMEM((2 * W, W), BF16),
            pltpu.VMEM((LEVELS - 1, PER, S, W), F32),
            pltpu.VMEM((LEVELS - 1, PER, S, W), F32),
            pltpu.VMEM((S, W), F32),
            pltpu.VMEM((S, W), F32),
            pltpu.VMEM((LEVELS - 1, PER, S, W), F32),
            pltpu.VMEM((PER, S, W), F32),
            pltpu.VMEM((PER, S, W), F32),
            dma((LEVELS + 1,)),
            dma,
            dma((LEVELS - 1, 3)),
            dma((LEVELS - 1,)),
            dma,
            dma((LEVELS - 1,)),
            dma,
            dma((LEVELS - 1,)),
            dma((2,)),
            dma((2,)),
        ],
        compiler_params=pltpu.CompilerParams(collective_id=0, has_side_effects=True, vmem_limit_bytes=60 * 2**20),
        name="solve",
    )(factor, pattern.reshape(1, LEVELS), inverse, rhs)


def solution(mesh):
    return jax.shard_map(
        shards,
        mesh=mesh,
        in_specs=(
            P(None, "row", None, "col", None, None),
            P(None, "row", None, "col"),
            P(),
            P(None, "row", None, None),
        ),
        out_specs=(P(None, "row", None, None), P(None, "row", None, None)),
        check_vma=False,
    )
```

time: 1700 us -> 53.8 us (0.03)
  waiting for transfers between devices: 1640 us -> 0 us
  Pallas kernels: 0 us -> 50 us
  matrix products: 27.5 us -> 0 us
    psum x16 -> x0, waiting for transfers between devices: 1640 us -> none  [the longest x4 555 us: forward(): picked = lax.psum(keeper * fresh, 'row')]
    pallas_call x0 -> x1, Pallas kernels: none -> 50 us  [shards(): pl.pallas_call(kernel, out_shape=(out, out), in_specs=[pl.BlockSpec(memor...]
    dot_general x16 -> x0, matrix products: 27.5 us -> none  [the longest x4 9.4 us: backward(): jnp.einsum('f,fcy,fch->yh', weight_matrix, factor_column_entries, owned_b...]
  transfers between devices with their start and end apart: 16 -> 0, of which waited for: 16 -> 0; matrix products, arithmetic and copies ran while one was open for 0% -> 0% of each run, Pallas kernels for 0% -> 0%
where the time goes in v1:
time: 53.8 us; the launch traced here: 53.6 us
  Pallas kernels  50 us (93%)
  local copies, waits for them, and re-layouts  2.95 us (5%)
  between operations  0.64 us (1%)
    pallas_call x1, Pallas kernels, shards(): pl.pallas_call(kernel, out_shape=(out, out), in_specs=[pl.BlockSpec(memor...  50 us
    unnamed x2, local copies, waits for them, and re-layouts  2.95 us

profile of v1, /device:TPU:1, one launch (start us, length us, event | category | flops | bytes accessed | tf_op | source)
XLA Modules:
  0.0 53.6 jit_solution(11281740170646765137)
XLA Ops:
  0.6 50.0 %solve.1 = (f32[1,1,128,128]{3,2,1,0:T(8,128)}, f32[1,1,128,128]{3,2,1,0:T(8,128)}) custom-call(f32[1,1,4,1,128,128]{5,4,3,2,1,0:T(8,128)} %factor.1, s32[1,4]{1,0:T(1,128)} %bitcast.1, f32[32,128,128]{2,1,0:T(8,128)} %inverse.1, f32[1,1,128,128]{3,2,1,0:T(8,128)} %rhs.1), custom_call_target="tpu_custom_call" | custom-call | tf_op jit(solution)/shard_map/solve/pallas_call | solution.py:184
  50.6 1.5 %copy.8 = f32[1,1,128,128]{3,2,1,0:T(8,128)} copy(f32[1,1,128,128]{3,2,1,0:T(8,128)} %get-tuple-element.4) | data formatting | bytes 131072
  52.1 1.5 %copy.9 = f32[1,1,128,128]{3,2,1,0:T(8,128)} copy(f32[1,1,128,128]{3,2,1,0:T(8,128)} %get-tuple-element.5) | data formatting | bytes 131072

commit v2 on v1

v2 whole, which is shorter than its diff:
```python
import jax
import jax.numpy as jnp
from jax import lax
from jax.experimental import pallas as pl
from jax.experimental.pallas import tpu as pltpu
from jax.sharding import PartitionSpec as P

MESH = pl.DeviceIdType.MESH
F32 = jnp.float32
BF16 = jnp.bfloat16
LEVELS = 4
PER = 8
W = 128
SLICES = 4
S = W // SLICES
FAR_FIRST = (4, 3, 5, 2, 6, 1, 7, 0)


def halves(v):
    hi = v.astype(BF16)
    lo = (v - hi.astype(F32)).astype(BF16)
    return hi, lo


def quadrants(p, m, n):
    return p[:m, :n] + (p[m:, :n] + p[:m, n:])


def dot_nt(a, b):
    return lax.dot_general(a, b, (((1,), (1,)), ((), ())), preferred_element_type=F32)


def dot_nn(a, b):
    return lax.dot_general(a, b, (((1,), (0,)), ((), ())), preferred_element_type=F32)


def kernel(
    factor, pattern, inverse, rhs, y_out, x_out,
    d_in, l_in, b_in, b_t, m_in, m_hl, d_hl, dt_hl, y_in, p_in, y_own, u_own, t_own, y_all, u_all,
    load_sem, m_send, m_recv, y_send, y_recv, p_send, p_recv, g_send, g_recv,
):
    row = lax.axis_index("row")
    col = lax.axis_index("col")
    level = row // PER
    z = row % PER
    x = col // 2
    solver = col % 2 == 1

    load_d = pltpu.make_async_copy(inverse.at[row], d_in, load_sem.at[0])
    load_b = pltpu.make_async_copy(rhs.at[0, 0], b_in, load_sem.at[1])
    load_l = [pltpu.make_async_copy(factor.at[0, 0, k, 0], l_in.at[k], load_sem.at[2 + k]) for k in range(LEVELS - 1)]
    load_d.start()
    load_l[0].start()

    def peer(dx, h):
        return lax.rem(x + dx, SLICES) * 2 + h

    barrier = pltpu.get_barrier_semaphore()

    def signal(to_row, to_col):
        pl.semaphore_signal(barrier, inc=1, device_id=(to_row, to_col), device_id_type=MESH)

    @pl.when(solver & (level > 0))
    def _():
        for dz in FAR_FIRST:
            signal(lax.rem(z + dz, PER), col)

    @pl.when(solver)
    def _():
        for dx in (2, 1, 3):
            signal(row, peer(dx, 1))
        for dx in (2, 1, 3, 0):
            signal(row, peer(dx, 0))

    @pl.when(jnp.logical_not(solver))
    def _():
        for dx in (2, 1, 3, 0):
            signal(row, peer(dx, 1))

    load_b.start()
    for k in range(1, LEVELS - 1):
        load_l[k].start()

    def wait(ref, sem):
        pltpu.make_async_copy(ref, ref, sem).wait()

    def send(src, dst, ssem, rsem, to_row, to_col):
        pltpu.make_async_remote_copy(
            src_ref=src, dst_ref=dst, send_sem=ssem, recv_sem=rsem, device_id=(to_row, to_col), device_id_type=MESH
        ).start()

    def to_level(src_of, dst, ssem, rsem, target):
        for dz in FAR_FIRST:
            zt = lax.rem(z + dz, PER)
            send(src_of(zt), dst, ssem, rsem, target * PER + zt, col)

    def to_row(own, all_, which):
        all_[x] = own[...]
        for dx, h in ((2, 0), (2, 1), (1, 0), (3, 0), (1, 1), (3, 1), (0, 0)):
            send(own, all_.at[x], g_send.at[which], g_recv.at[which], row, peer(dx, h))

    load_d.wait()
    dh_, dl_ = halves(d_in[...])
    d_hl[:W, :] = dh_
    d_hl[W:, :] = dl_

    def form(k):
        load_l[k].wait()
        lh, ll = halves(l_in[k] * pattern[0, k].astype(F32))
        m_in[k, col] = quadrants(dot_nn(d_hl[...], jnp.concatenate([lh, ll], axis=1)), W, W)

    def turn():
        th, tl = halves(jnp.transpose(d_in[...]))
        dt_hl[:W, :] = th
        dt_hl[W:, :] = tl

    def finish(messages):
        wait(y_all.at[pl.ds(0, messages)], g_recv.at[0])
        y_out[0, 0] = jnp.transpose(y_all[...].reshape(W, W))
        wait(u_all.at[pl.ds(0, messages)], g_recv.at[1])
        ah, al = halves(u_all[...].reshape(W, W))
        x_out[0, 0] = quadrants(dot_nt(dt_hl[...], jnp.concatenate([ah, al], axis=0)), W, W)

    @pl.when(jnp.logical_not(solver))
    def _():
        for k in range(LEVELS - 1):

            @pl.when(level > k)
            def _(k=k):
                form(k)
                if k == 0:
                    pl.semaphore_wait(barrier, SLICES)
                own = m_in.at[k, col]
                for dx in (2, 1, 3, 0):
                    send(own, own, m_send, m_recv.at[k], row, peer(dx, 1))

            @pl.when(level <= k)
            def _(k=k):
                load_l[k].wait()

        @pl.when(level == 0)
        def _():
            pl.semaphore_wait(barrier, SLICES)

        load_b.wait()
        turn()
        finish(SLICES)
        for k in range(LEVELS - 1):

            @pl.when(level > k)
            def _(k=k):
                wait(m_in.at[k, pl.ds(0, SLICES)], m_send)

    def first_term():
        load_b.wait()
        b_t[...] = jnp.transpose(b_in[...])
        bh, bl = halves(b_t[pl.ds(pl.multiple_of(x * S, S), S), :])
        return quadrants(dot_nt(jnp.concatenate([bh, bl], axis=0), d_hl[...]), S, W)

    for lev in range(LEVELS):

        @pl.when(solver & (level == lev))
        def _(lev=lev):
            if lev == 0:
                start = first_term()
                y_own[...] = start
                pl.semaphore_wait(barrier, 31)
                for target in range(1, LEVELS):
                    to_level(lambda zt: y_own, y_in.at[0, z], y_send, y_recv.at[0], target)
            for k in range(lev, LEVELS - 1):
                load_l[k].wait()
            for k in range(lev):
                form(k)
                if k == 0:
                    pl.semaphore_wait(barrier, 7)
                own = m_in.at[k, col]
                for dx in (2, 1, 3):
                    send(own, own, m_send, m_recv.at[k], row, peer(dx, 1))
            if lev > 0:
                start = first_term()
            turn()
            for k in range(lev):
                wait(m_in.at[k, pl.ds(0, PER - 1)], m_recv.at[k])
                for c in range(PER):
                    mh, ml = halves(m_in[k, c])
                    m_hl[k, :W, c * W:(c + 1) * W] = mh
                    m_hl[k, W:, c * W:(c + 1) * W] = ml
            acc = start
            for k in range(lev):
                wait(y_in.at[k], y_recv.at[k])
                parts = [halves(y_in[k, c]) for c in range(PER)]
                lhs = jnp.concatenate(
                    [jnp.concatenate([p[0] for p in parts], axis=1), jnp.concatenate([p[1] for p in parts], axis=1)], axis=0
                )
                acc = acc - quadrants(dot_nt(lhs, m_hl[k]), S, W)
            if lev > 0:
                y_own[...] = acc
                for target in range(lev + 1, LEVELS):
                    to_level(lambda zt: y_own, y_in.at[lev, z], y_send, y_recv.at[lev], target)
            if lev < LEVELS - 1:
                to_row(y_own, y_all, 0)
            for up in range(LEVELS - 1, lev, -1):
                wait(p_in.at[up - 1], p_recv.at[up - 1])
                total = p_in[up - 1, 0]
                for c in range(1, PER):
                    total = total + p_in[up - 1, c]
                acc = acc - total
            u_own[...] = acc
            uh, ul = halves(acc)
            lhs = jnp.concatenate(
                [jnp.concatenate([uh, uh], axis=1), jnp.concatenate([ul, jnp.zeros_like(ul)], axis=1)], axis=0
            )
            for k in range(lev - 1, -1, -1):
                t = dot_nn(lhs, m_hl[k])
                t = t[:S] + t[S:]
                for c in range(PER):
                    t_own[k, c] = t[:, c * W:(c + 1) * W]
                to_level(lambda zt: t_own.at[k, zt], p_in.at[lev - 1, z], p_send, p_recv.at[lev - 1], k)
            if lev == LEVELS - 1:
                to_row(y_own, y_all, 0)
            to_row(u_own, u_all, 1)
            finish(SLICES - 1)

            for k in range(lev):
                wait(m_in.at[k, pl.ds(0, SLICES - 1)], m_send)
                wait(t_own.at[k], p_send)
            for _ in range(lev + 1, LEVELS):
                wait(y_in.at[0], y_send)
            for which in range(2):
                wait(y_in.at[0, pl.ds(0, 7)], g_send.at[which])


def put(y, x, y_out, x_out, sem):
    a = pltpu.make_async_copy(y, y_out, sem.at[0])
    b = pltpu.make_async_copy(x, x_out, sem.at[1])
    a.start()
    b.start()
    a.wait()
    b.wait()


def shards(factor, pattern, inverse, rhs):
    out = jax.ShapeDtypeStruct((1, 1, W, W), F32)
    dma = pltpu.SemaphoreType.DMA
    y, x = pl.pallas_call(
        kernel,
        out_shape=(out, out),
        in_specs=[
            pl.BlockSpec(memory_space=pltpu.HBM),
            pl.BlockSpec(memory_space=pltpu.SMEM),
            pl.BlockSpec(memory_space=pltpu.HBM),
            pl.BlockSpec(memory_space=pltpu.HBM),
        ],
        out_specs=(pl.BlockSpec(memory_space=pltpu.VMEM), pl.BlockSpec(memory_space=pltpu.VMEM)),
        scratch_shapes=[
            pltpu.VMEM((W, W), F32),
            pltpu.VMEM((LEVELS - 1, W, W), F32),
            pltpu.VMEM((W, W), F32),
            pltpu.VMEM((W, W), F32),
            pltpu.VMEM((LEVELS - 1, PER, W, W), F32),
            pltpu.VMEM((LEVELS - 1, 2 * W, PER * W), BF16),
            pltpu.VMEM((2 * W, W), BF16),
            pltpu.VMEM((2 * W, W), BF16),
            pltpu.VMEM((LEVELS - 1, PER, S, W), F32),
            pltpu.VMEM((LEVELS - 1, PER, S, W), F32),
            pltpu.VMEM((S, W), F32),
            pltpu.VMEM((S, W), F32),
            pltpu.VMEM((LEVELS - 1, PER, S, W), F32),
            pltpu.VMEM((SLICES, S, W), F32),
            pltpu.VMEM((SLICES, S, W), F32),
            dma((LEVELS + 1,)),
            dma,
            dma((LEVELS - 1,)),
            dma,
            dma((LEVELS - 1,)),
            dma,
            dma((LEVELS - 1,)),
            dma((2,)),
            dma((2,)),
        ],
        compiler_params=pltpu.CompilerParams(collective_id=0, has_side_effects=True, vmem_limit_bytes=60 * 2**20),
        name="solve",
    )(factor, pattern.reshape(1, LEVELS), inverse, rhs)
    return pl.pallas_call(
        put,
        out_shape=(out, out),
        in_specs=[pl.BlockSpec(memory_space=pltpu.VMEM)] * 2,
        out_specs=(pl.BlockSpec(memory_space=pltpu.HBM),) * 2,
        scratch_shapes=[dma((2,))],
        name="put",
    )(y, x)


def solution(mesh):
    return jax.shard_map(
        shards,
        mesh=mesh,
        in_specs=(
            P(None, "row", None, "col", None, None),
            P(None, "row", None, "col"),
            P(),
            P(None, "row", None, None),
        ),
        out_specs=(P(None, "row", None, None), P(None, "row", None, None)),
        check_vma=False,
    )
```

time: 53.8 us -> 47.5 us (0.88)
  Pallas kernels: 50 us -> 46.7 us
  local copies, waits for them, and re-layouts: 2.95 us -> 0 us
    pallas_call x1, Pallas kernels: 50 us -> 45.2 us  [shards(): pl.pallas_call(kernel, out_shape=(out, out), in_specs=[pl.BlockSpec(memor...]
    unnamed x2 -> x0, local copies, waits for them, and re-layouts: 2.95 us -> none
    pallas_call x0 -> x1, Pallas kernels: none -> 1.54 us  [shards(): pl.pallas_call(put, out_shape=(out, out), in_specs=[pl.BlockSpec(memory_s...]
where the time goes in v2:
time: 47.5 us; the launch traced here: 47.4 us
  Pallas kernels  46.7 us (98%)
  between operations  0.64 us (1%)
    pallas_call x1, Pallas kernels, shards(): pl.pallas_call(kernel, out_shape=(out, out), in_specs=[pl.BlockSpec(memor...  45.2 us
    pallas_call x1, Pallas kernels, shards(): pl.pallas_call(put, out_shape=(out, out), in_specs=[pl.BlockSpec(memory_s...  1.54 us

profile of v2, /device:TPU:1, one launch (start us, length us, event | category | flops | bytes accessed | tf_op | source)
XLA Modules:
  0.0 47.4 jit_solution(7569137776722706799)
XLA Ops:
  0.6 45.2 %solve.1 = (f32[1,1,128,128]{3,2,1,0:T(8,128)}, f32[1,1,128,128]{3,2,1,0:T(8,128)}) custom-call(f32[1,1,4,1,128,128]{5,4,3,2,1,0:T(8,128)} %factor.1, s32[1,4]{1,0:T(1,128)} %bitcast.1, f32[32,128,128]{2,1,0:T(8,128)} %inverse.1, f32[1,1,128,128]{3,2,1,0:T(8,128)} %rhs.1), custom_call_target="tpu_custom_call" | custom-call | tf_op jit(solution)/shard_map/solve/pallas_call | solution.py:245
  45.8 1.5 %put.1 = (f32[1,1,128,128]{3,2,1,0:T(8,128)}, f32[1,1,128,128]{3,2,1,0:T(8,128)}) custom-call(f32[1,1,128,128]{3,2,1,0:T(8,128)} %get-tuple-element.4.y, f32[1,1,128,128]{3,2,1,0:T(8,128)} %get-tuple-element.5.x), custom_call_target="tpu_custom_call" | custom-call | tf_op jit(solution)/shard_map/put/pallas_call | solution.py:284

commit v3 on v2

--- a/solution.py
+++ b/solution.py
@@ -36,8 +36,8 @@
 
 def kernel(
     factor, pattern, inverse, rhs, y_out, x_out,
-    d_in, l_in, b_in, b_t, m_in, m_hl, d_hl, dt_hl, y_in, p_in, y_own, u_own, t_own, y_all, u_all,
-    load_sem, m_send, m_recv, y_send, y_recv, p_send, p_recv, g_send, g_recv,
+    d_in, l_in, b_in, b_t, m_in, m_fwd, m_bwd, d_hl, dt_hl, y_in, p_in, y_own, u_own, t_own, y_all, u_all,
+    go, load_sem, m_send, m_recv, y_send, y_recv, p_send, p_recv, g_send, g_recv,
 ):
     row = lax.axis_index("row")
     col = lax.axis_index("col")
@@ -60,10 +60,15 @@
     def signal(to_row, to_col):
         pl.semaphore_signal(barrier, inc=1, device_id=(to_row, to_col), device_id_type=MESH)
 
+    @pl.when(solver & (level == 1))
+    def _():
+        for dz in FAR_FIRST:
+            signal(lax.rem(z + dz, PER), peer(0, 1))
+
     @pl.when(solver & (level > 0))
     def _():
         for dz in FAR_FIRST:
-            signal(lax.rem(z + dz, PER), col)
+            signal(lax.rem(z + dz, PER), peer(0, 0))
 
     @pl.when(solver)
     def _():
@@ -140,7 +145,9 @@
 
         @pl.when(level == 0)
         def _():
-            pl.semaphore_wait(barrier, SLICES)
+            pl.semaphore_wait(barrier, SLICES + 3 * PER)
+            for to in (row, PER + row):
+                pl.semaphore_signal(go, inc=1, device_id=(to, peer(0, 1)), device_id_type=MESH)
 
         load_b.wait()
         turn()
@@ -164,8 +171,10 @@
             if lev == 0:
                 start = first_term()
                 y_own[...] = start
-                pl.semaphore_wait(barrier, 31)
+                pl.semaphore_wait(barrier, 7 + PER)
                 for target in range(1, LEVELS):
+                    if target == 2:
+                        pl.semaphore_wait(go, 1)
                     to_level(lambda zt: y_own, y_in.at[0, z], y_send, y_recv.at[0], target)
             for k in range(lev, LEVELS - 1):
                 load_l[k].wait()
@@ -182,9 +191,9 @@
             for k in range(lev):
                 wait(m_in.at[k, pl.ds(0, PER - 1)], m_recv.at[k])
                 for c in range(PER):
-                    mh, ml = halves(m_in[k, c])
-                    m_hl[k, :W, c * W:(c + 1) * W] = mh
-                    m_hl[k, W:, c * W:(c + 1) * W] = ml
+                    mh, ml = halves(jnp.transpose(m_in[k, c]))
+                    m_fwd[k, c * W:(c + 1) * W, :W] = mh
+                    m_fwd[k, c * W:(c + 1) * W, W:] = ml
             acc = start
             for k in range(lev):
                 wait(y_in.at[k], y_recv.at[k])
@@ -192,13 +201,20 @@
                 lhs = jnp.concatenate(
                     [jnp.concatenate([p[0] for p in parts], axis=1), jnp.concatenate([p[1] for p in parts], axis=1)], axis=0
                 )
-                acc = acc - quadrants(dot_nt(lhs, m_hl[k]), S, W)
+                acc = acc - quadrants(dot_nn(lhs, m_fwd[k]), S, W)
             if lev > 0:
                 y_own[...] = acc
+                if lev == 1:
+                    pl.semaphore_wait(go, 1)
                 for target in range(lev + 1, LEVELS):
                     to_level(lambda zt: y_own, y_in.at[lev, z], y_send, y_recv.at[lev], target)
             if lev < LEVELS - 1:
                 to_row(y_own, y_all, 0)
+            for k in range(lev):
+                for c in range(PER):
+                    mh, ml = halves(m_in[k, c])
+                    m_bwd[k, :W, c * W:(c + 1) * W] = mh
+                    m_bwd[k, W:, c * W:(c + 1) * W] = ml
             for up in range(LEVELS - 1, lev, -1):
                 wait(p_in.at[up - 1], p_recv.at[up - 1])
                 total = p_in[up - 1, 0]
@@ -211,7 +227,7 @@
                 [jnp.concatenate([uh, uh], axis=1), jnp.concatenate([ul, jnp.zeros_like(ul)], axis=1)], axis=0
             )
             for k in range(lev - 1, -1, -1):
-                t = dot_nn(lhs, m_hl[k])
+                t = dot_nn(lhs, m_bwd[k])
                 t = t[:S] + t[S:]
                 for c in range(PER):
                     t_own[k, c] = t[:, c * W:(c + 1) * W]
@@ -258,6 +274,7 @@
             pltpu.VMEM((W, W), F32),
             pltpu.VMEM((W, W), F32),
             pltpu.VMEM((LEVELS - 1, PER, W, W), F32),
+            pltpu.VMEM((LEVELS - 1, PER * W, 2 * W), BF16),
             pltpu.VMEM((LEVELS - 1, 2 * W, PER * W), BF16),
             pltpu.VMEM((2 * W, W), BF16),
             pltpu.VMEM((2 * W, W), BF16),
@@ -268,6 +285,7 @@
             pltpu.VMEM((LEVELS - 1, PER, S, W), F32),
             pltpu.VMEM((SLICES, S, W), F32),
             pltpu.VMEM((SLICES, S, W), F32),
+            pltpu.SemaphoreType.REGULAR,
             dma((LEVELS + 1,)),
             dma,
             dma((LEVELS - 1,)),

time: 47.5 us -> 45.7 us (0.962)
  Pallas kernels: 46.7 us -> 44.9 us
    pallas_call x1, Pallas kernels: 45.2 us -> 43.3 us  [shards(): pl.pallas_call(kernel, out_shape=(out, out), in_specs=[pl.BlockSpec(memor...]
where the time goes in v3:
time: 45.7 us; the launch traced here: 45.5 us
  Pallas kernels  44.9 us (98%)
  between operations  0.64 us (1%)
    pallas_call x1, Pallas kernels, shards(): pl.pallas_call(kernel, out_shape=(out, out), in_specs=[pl.BlockSpec(memor...  43.3 us
    pallas_call x1, Pallas kernels, shards(): pl.pallas_call(put, out_shape=(out, out), in_specs=[pl.BlockSpec(memory_s...  1.54 us

profile of v3, /device:TPU:1, one launch (start us, length us, event | category | flops | bytes accessed | tf_op | source)
XLA Modules:
  0.0 45.5 jit_solution(2707912328306960454)
XLA Ops:
  0.6 43.3 %solve.1 = (f32[1,1,128,128]{3,2,1,0:T(8,128)}, f32[1,1,128,128]{3,2,1,0:T(8,128)}) custom-call(f32[1,1,4,1,128,128]{5,4,3,2,1,0:T(8,128)} %factor.1, s32[1,4]{1,0:T(1,128)} %bitcast.1, f32[32,128,128]{2,1,0:T(8,128)} %inverse.1, f32[1,1,128,128]{3,2,1,0:T(8,128)} %rhs.1), custom_call_target="tpu_custom_call" | custom-call | tf_op jit(solution)/shard_map/solve/pallas_call | solution.py:261
  44.0 1.5 %put.1 = (f32[1,1,128,128]{3,2,1,0:T(8,128)}, f32[1,1,128,128]{3,2,1,0:T(8,128)}) custom-call(f32[1,1,128,128]{3,2,1,0:T(8,128)} %get-tuple-element.4.y, f32[1,1,128,128]{3,2,1,0:T(8,128)} %get-tuple-element.5.x), custom_call_target="tpu_custom_call" | custom-call | tf_op jit(solution)/shard_map/put/pallas_call | solution.py:302

commit v4 on v3

--- a/solution.py
+++ b/solution.py
@@ -94,10 +94,16 @@
             src_ref=src, dst_ref=dst, send_sem=ssem, recv_sem=rsem, device_id=(to_row, to_col), device_id_type=MESH
         ).start()
 
-    def to_level(src_of, dst, ssem, rsem, target):
-        for dz in FAR_FIRST:
-            zt = lax.rem(z + dz, PER)
-            send(src_of(zt), dst, ssem, rsem, target * PER + zt, col)
+    def to_level(src_of, dst, ssem, rsem, target, slots=range(PER)):
+        for i in slots:
+            zt = lax.rem(z + FAR_FIRST[i], PER)
+            send(src_of(i), dst.at[i], ssem, rsem.at[min(i, 1)], target * PER + zt, col)
+
+    def wait_near(ref, sem):
+        wait(ref.at[pl.ds(1, PER - 1)], sem.at[1])
+
+    def wait_far(ref, sem):
+        wait(ref.at[0], sem.at[0])
 
     def to_row(own, all_, which):
         all_[x] = own[...]
@@ -175,7 +181,7 @@
                 for target in range(1, LEVELS):
                     if target == 2:
                         pl.semaphore_wait(go, 1)
-                    to_level(lambda zt: y_own, y_in.at[0, z], y_send, y_recv.at[0], target)
+                    to_level(lambda i: y_own, y_in.at[0], y_send, y_recv.at[0], target)
             for k in range(lev, LEVELS - 1):
                 load_l[k].wait()
             for k in range(lev):
@@ -190,37 +196,42 @@
             turn()
             for k in range(lev):
                 wait(m_in.at[k, pl.ds(0, PER - 1)], m_recv.at[k])
-                for c in range(PER):
-                    mh, ml = halves(jnp.transpose(m_in[k, c]))
-                    m_fwd[k, c * W:(c + 1) * W, :W] = mh
-                    m_fwd[k, c * W:(c + 1) * W, W:] = ml
+                for i in range(PER):
+                    mh, ml = halves(jnp.transpose(m_in[k, lax.rem(z + PER - FAR_FIRST[i], PER)]))
+                    m_fwd[k, i * W:(i + 1) * W, :W] = mh
+                    m_fwd[k, i * W:(i + 1) * W, W:] = ml
             acc = start
             for k in range(lev):
-                wait(y_in.at[k], y_recv.at[k])
-                parts = [halves(y_in[k, c]) for c in range(PER)]
+                wait_near(y_in.at[k], y_recv.at[k])
+                parts = [halves(y_in[k, i]) for i in range(1, PER)]
                 lhs = jnp.concatenate(
                     [jnp.concatenate([p[0] for p in parts], axis=1), jnp.concatenate([p[1] for p in parts], axis=1)], axis=0
                 )
-                acc = acc - quadrants(dot_nn(lhs, m_fwd[k]), S, W)
+                acc = acc - quadrants(dot_nn(lhs, m_fwd[k, W:]), S, W)
+                wait_far(y_in.at[k], y_recv.at[k])
+                lhs = jnp.concatenate(halves(y_in[k, 0]), axis=0)
+                acc = acc - quadrants(dot_nn(lhs, m_fwd[k, :W]), S, W)
             if lev > 0:
                 y_own[...] = acc
                 if lev == 1:
                     pl.semaphore_wait(go, 1)
                 for target in range(lev + 1, LEVELS):
-                    to_level(lambda zt: y_own, y_in.at[lev, z], y_send, y_recv.at[lev], target)
+                    to_level(lambda i: y_own, y_in.at[lev], y_send, y_recv.at[lev], target)
             if lev < LEVELS - 1:
                 to_row(y_own, y_all, 0)
             for k in range(lev):
-                for c in range(PER):
-                    mh, ml = halves(m_in[k, c])
-                    m_bwd[k, :W, c * W:(c + 1) * W] = mh
-                    m_bwd[k, W:, c * W:(c + 1) * W] = ml
+                for i in range(PER):
+                    mh, ml = halves(m_in[k, lax.rem(z + FAR_FIRST[i], PER)])
+                    m_bwd[k, :W, i * W:(i + 1) * W] = mh
+                    m_bwd[k, W:, i * W:(i + 1) * W] = ml
             for up in range(LEVELS - 1, lev, -1):
-                wait(p_in.at[up - 1], p_recv.at[up - 1])
-                total = p_in[up - 1, 0]
-                for c in range(1, PER):
-                    total = total + p_in[up - 1, c]
+                wait_near(p_in.at[up - 1], p_recv.at[up - 1])
+                total = p_in[up - 1, 1]
+                for i in range(2, PER):
+                    total = total + p_in[up - 1, i]
                 acc = acc - total
+                wait_far(p_in.at[up - 1], p_recv.at[up - 1])
+                acc = acc - p_in[up - 1, 0]
             u_own[...] = acc
             uh, ul = halves(acc)
             lhs = jnp.concatenate(
@@ -231,7 +242,7 @@
                 t = t[:S] + t[S:]
                 for c in range(PER):
                     t_own[k, c] = t[:, c * W:(c + 1) * W]
-                to_level(lambda zt: t_own.at[k, zt], p_in.at[lev - 1, z], p_send, p_recv.at[lev - 1], k)
+                to_level(lambda i: t_own.at[k, i], p_in.at[lev - 1], p_send, p_recv.at[lev - 1], k)
             if lev == LEVELS - 1:
                 to_row(y_own, y_all, 0)
             to_row(u_own, u_all, 1)
@@ -290,9 +301,9 @@
             dma,
             dma((LEVELS - 1,)),
             dma,
-            dma((LEVELS - 1,)),
+            dma((LEVELS - 1, 2)),
             dma,
-            dma((LEVELS - 1,)),
+            dma((LEVELS - 1, 2)),
             dma((2,)),
             dma((2,)),
         ],

time: 45.7 us -> 45.4 us (level)
  no operation moved by 1% of the time
where the time goes in v4:
time: 45.4 us; the launch traced here: 45.2 us
  Pallas kernels  44.5 us (98%)
  between operations  0.64 us (1%)
    pallas_call x1, Pallas kernels, shards(): pl.pallas_call(kernel, out_shape=(out, out), in_specs=[pl.BlockSpec(memor...  43 us
    pallas_call x1, Pallas kernels, shards(): pl.pallas_call(put, out_shape=(out, out), in_specs=[pl.BlockSpec(memory_s...  1.54 us

profile of v4, /device:TPU:1, one launch (start us, length us, event | category | flops | bytes accessed | tf_op | source)
XLA Modules:
  0.0 45.2 jit_solution(4482481063236122030)
XLA Ops:
  0.6 43.0 %solve.1 = (f32[1,1,128,128]{3,2,1,0:T(8,128)}, f32[1,1,128,128]{3,2,1,0:T(8,128)}) custom-call(f32[1,1,4,1,128,128]{5,4,3,2,1,0:T(8,128)} %factor.1, s32[1,4]{1,0:T(1,128)} %bitcast.1, f32[32,128,128]{2,1,0:T(8,128)} %inverse.1, f32[1,1,128,128]{3,2,1,0:T(8,128)} %rhs.1), custom_call_target="tpu_custom_call" | custom-call | tf_op jit(solution)/shard_map/solve/pallas_call | solution.py:272
  43.6 1.5 %put.1 = (f32[1,1,128,128]{3,2,1,0:T(8,128)}, f32[1,1,128,128]{3,2,1,0:T(8,128)}) custom-call(f32[1,1,128,128]{3,2,1,0:T(8,128)} %get-tuple-element.4.y, f32[1,1,128,128]{3,2,1,0:T(8,128)} %get-tuple-element.5.x), custom_call_target="tpu_custom_call" | custom-call | tf_op jit(solution)/shard_map/put/pallas_call | solution.py:313

commit v5 on v4

--- a/solution.py
+++ b/solution.py
@@ -271,7 +271,7 @@
     dma = pltpu.SemaphoreType.DMA
     y, x = pl.pallas_call(
         kernel,
-        out_shape=(out, out),
+        out_shape=(pltpu.VMEM((1, 1, W, W), F32),) * 2,
         in_specs=[
             pl.BlockSpec(memory_space=pltpu.HBM),
             pl.BlockSpec(memory_space=pltpu.SMEM),
@@ -317,7 +317,7 @@
         out_specs=(pl.BlockSpec(memory_space=pltpu.HBM),) * 2,
         scratch_shapes=[dma((2,))],
         name="put",
-    )(y, x)
+    )(pltpu.with_memory_space_constraint(y, pltpu.VMEM), pltpu.with_memory_space_constraint(x, pltpu.VMEM))
 
 
 def solution(mesh):

time: 45.4 us -> 43.8 us (0.965)
  Pallas kernels: 44.5 us -> 43 us
    pallas_call x1, Pallas kernels: 1.54 us -> 0.67 us  [shards(): pl.pallas_call(put, out_shape=(out, out), in_specs=[pl.BlockSpec(memory_s...]
    pallas_call x1, Pallas kernels: 43 us -> 42.3 us  [shards(): pl.pallas_call(kernel, out_shape=(pltpu.VMEM((1, 1, W, W), F32),) * 2, in...]
where the time goes in v5:
time: 43.8 us; the launch traced here: 43.6 us
  Pallas kernels  43 us (98%)
  between operations  0.64 us (1%)
    pallas_call x1, Pallas kernels, shards(): pl.pallas_call(kernel, out_shape=(pltpu.VMEM((1, 1, W, W), F32),) * 2, in...  42.3 us

profile of v5, /device:TPU:1, one launch (start us, length us, event | category | flops | bytes accessed | tf_op | source)
XLA Modules:
  0.0 43.6 jit_solution(7218961365649886779)
XLA Ops:
  0.6 42.3 %solve.1 = (f32[1,1,128,128]{3,2,1,0:T(8,128)S(1)}, f32[1,1,128,128]{3,2,1,0:T(8,128)S(1)}) custom-call(f32[1,1,4,1,128,128]{5,4,3,2,1,0:T(8,128)} %factor.1, s32[1,4]{1,0:T(1,128)} %bitcast.1, f32[32,128,128]{2,1,0:T(8,128)} %inverse.1, f32[1,1,128,128]{3,2,1,0:T(8,128)} %rhs.1), custom_call_target="tpu_custom_call" | custom-call | tf_op jit(solution)/shard_map/solve/pallas_call | solution.py:272
  43.0 0.7 %put.1 = (f32[1,1,128,128]{3,2,1,0:T(8,128)}, f32[1,1,128,128]{3,2,1,0:T(8,128)}) custom-call(f32[1,1,128,128]{3,2,1,0:T(8,128)S(1)} %get-tuple-element.4.y, f32[1,1,128,128]{3,2,1,0:T(8,128)S(1)} %get-tuple-element.5.x), custom_call_target="tpu_custom_call" | custom-call | tf_op jit(solution)/shard_map/put/pallas_call | solution.py:313

commit v6 on v5

--- a/solution.py
+++ b/solution.py
@@ -37,7 +37,7 @@
 def kernel(
     factor, pattern, inverse, rhs, y_out, x_out,
     d_in, l_in, b_in, b_t, m_in, m_fwd, m_bwd, d_hl, dt_hl, y_in, p_in, y_own, u_own, t_own, y_all, u_all,
-    go, load_sem, m_send, m_recv, y_send, y_recv, p_send, p_recv, g_send, g_recv,
+    kept, go, load_sem, m_send, m_recv, y_send, y_recv, p_send, p_recv, g_send, g_recv,
 ):
     row = lax.axis_index("row")
     col = lax.axis_index("col")
@@ -49,8 +49,10 @@
     load_d = pltpu.make_async_copy(inverse.at[row], d_in, load_sem.at[0])
     load_b = pltpu.make_async_copy(rhs.at[0, 0], b_in, load_sem.at[1])
     load_l = [pltpu.make_async_copy(factor.at[0, 0, k, 0], l_in.at[k], load_sem.at[2 + k]) for k in range(LEVELS - 1)]
+    load_p = pltpu.make_async_copy(pattern, kept, load_sem.at[LEVELS + 1])
     load_d.start()
     load_l[0].start()
+    load_p.start()
 
     def peer(dx, h):
         return lax.rem(x + dx, SLICES) * 2 + h
@@ -110,6 +112,7 @@
         for dx, h in ((2, 0), (2, 1), (1, 0), (3, 0), (1, 1), (3, 1), (0, 0)):
             send(own, all_.at[x], g_send.at[which], g_recv.at[which], row, peer(dx, h))
 
+    load_p.wait()
     load_d.wait()
     dh_, dl_ = halves(d_in[...])
     d_hl[:W, :] = dh_
@@ -117,7 +120,7 @@
 
     def form(k):
         load_l[k].wait()
-        lh, ll = halves(l_in[k] * pattern[0, k].astype(F32))
+        lh, ll = halves(l_in[k] * kept[0, k].astype(F32))
         m_in[k, col] = quadrants(dot_nn(d_hl[...], jnp.concatenate([lh, ll], axis=1)), W, W)
 
     def turn():
@@ -274,7 +277,7 @@
         out_shape=(pltpu.VMEM((1, 1, W, W), F32),) * 2,
         in_specs=[
             pl.BlockSpec(memory_space=pltpu.HBM),
-            pl.BlockSpec(memory_space=pltpu.SMEM),
+            pl.BlockSpec(memory_space=pltpu.HBM),
             pl.BlockSpec(memory_space=pltpu.HBM),
             pl.BlockSpec(memory_space=pltpu.HBM),
         ],
@@ -296,8 +299,9 @@
             pltpu.VMEM((LEVELS - 1, PER, S, W), F32),
             pltpu.VMEM((SLICES, S, W), F32),
             pltpu.VMEM((SLICES, S, W), F32),
+            pltpu.SMEM((1, LEVELS), jnp.int32),
             pltpu.SemaphoreType.REGULAR,
-            dma((LEVELS + 1,)),
+            dma((LEVELS + 2,)),
             dma,
             dma((LEVELS - 1,)),
             dma,

time: 43.8 us -> 43.1 us (0.984)
  Pallas kernels: 43 us -> 42.3 us
    pallas_call x1, Pallas kernels: 42.3 us -> 41.7 us  [shards(): pl.pallas_call(kernel, out_shape=(pltpu.VMEM((1, 1, W, W), F32),) * 2, in...]
where the time goes in v6:
time: 43.1 us; the launch traced here: 43 us
  Pallas kernels  42.3 us (98%)
  between operations  0.64 us (1%)
    pallas_call x1, Pallas kernels, shards(): pl.pallas_call(kernel, out_shape=(pltpu.VMEM((1, 1, W, W), F32),) * 2, in...  41.7 us

profile of v6, /device:TPU:1, one launch (start us, length us, event | category | flops | bytes accessed | tf_op | source)
XLA Modules:
  0.0 43.0 jit_solution(8185732657938260295)
XLA Ops:
  0.6 41.7 %solve.1 = (f32[1,1,128,128]{3,2,1,0:T(8,128)S(1)}, f32[1,1,128,128]{3,2,1,0:T(8,128)S(1)}) custom-call(f32[1,1,4,1,128,128]{5,4,3,2,1,0:T(8,128)} %factor.1, s32[1,4]{1,0:T(1,128)} %bitcast.1, f32[32,128,128]{2,1,0:T(8,128)} %inverse.1, f32[1,1,128,128]{3,2,1,0:T(8,128)} %rhs.1), custom_call_target="tpu_custom_call" | custom-call | tf_op jit(solution)/shard_map/solve/pallas_call | solution.py:275
  42.3 0.7 %put.1 = (f32[1,1,128,128]{3,2,1,0:T(8,128)}, f32[1,1,128,128]{3,2,1,0:T(8,128)}) custom-call(f32[1,1,128,128]{3,2,1,0:T(8,128)S(1)} %get-tuple-element.4.y, f32[1,1,128,128]{3,2,1,0:T(8,128)S(1)} %get-tuple-element.5.x), custom_call_target="tpu_custom_call" | custom-call | tf_op jit(solution)/shard_map/put/pallas_call | solution.py:317
